TPU v7x, 32 devices: a whole 2x2x4 slice. The times are simulated.
32 devices in a mesh: pair: 4 (over x, core), virt: 4 (over z), ksplit: 2 (over y).
Axes of the slice: x: 2, y: 2, z: 4, core: 2. Of those that a mesh axis runs over, the one named last changes fastest.
Arguments:
- weights: bfloat16 [1024, 1024], P('virt', 'ksplit'), may hold values from -0.1875 to 0.1875
- amplitudes: bfloat16 [32, 2, 4, 128, 128], P(('pair', 'virt'), 'ksplit'), may hold values from -6 to 6
- slot_tiles: int32 [32, 2, 4], P(('pair', 'virt'), 'ksplit'), may hold values from 0 to 7, as said below
- slot_counts: int32 [32, 2], P(('pair', 'virt'), 'ksplit'), may hold values from 1 to 4
- driving: bfloat16 [32, 1024, 128], P(('pair', 'ksplit'), 'virt'), may hold values from -6 to 6
- virt_energy: float32 [1024], replicated, may hold values from 0.5 to 3
- pair_energy: float32 [32], P(('pair', 'ksplit')), may hold values from -3 to -1
- pair_tile: int32 [32], P(('pair', 'ksplit')), may hold values from 0 to 7
Outputs:
- regrouped: bfloat16 [32, 128, 1024], P(('pair', 'ksplit'), 'virt')
Inputs may be any that keep to these rules, and one draw needn't show every extreme that they name: slot_tiles[p, k, s] lies in block k: from k * 4 to (k + 1) * 4 - 1.
All inputs are finite; a program needn't handle non-finite values.
Results may differ from a plain program's by a relative error of at most 0.0065.
Values may be sent and summed in bfloat16 or wider, within the bound.
A program may use at most 128 MiB of HBM per device.

v0:
```python
import jax
import jax.numpy as jnp
from jax import lax
from jax.sharding import PartitionSpec as P


def body(
    weights, amplitudes, slot_tiles, slot_counts, driving, virt_energy, pair_energy, pair_tile
):
    tile_width = amplitudes.shape[-1]
    slot_number = amplitudes.shape[2]
    rows_local = weights.shape[0]
    blocks_local = weights.shape[1] // tile_width
    split_index = lax.axis_index("ksplit")
    virt_index = lax.axis_index("virt")
    column_tiles = weights.reshape(rows_local, blocks_local, tile_width)
    amps = lax.all_gather(amplitudes, "virt", axis=0, tiled=True)
    tiles = lax.all_gather(slot_tiles, "virt", axis=0, tiled=True)
    counts = lax.all_gather(slot_counts, "virt", axis=0, tiled=True)
    local_ids = tiles[:, 0, :] - split_index * blocks_local
    chosen = jnp.take(column_tiles, local_ids, axis=1)
    live_slot = jnp.arange(slot_number, dtype=jnp.int32)[None, :] < counts
    masked = jnp.where(live_slot[:, :, None, None], amps[:, 0], jnp.zeros((), jnp.bfloat16))
    partial_value = jnp.einsum("apsc,pscb->pab", chosen, masked, preferred_element_type=jnp.float32)
    tile_count = virt_energy.shape[0] // tile_width
    energy_table = virt_energy.reshape(tile_count, tile_width)
    one_hot = (pair_tile[:, None] == jnp.arange(tile_count, dtype=jnp.int32)[None, :]).astype(
        jnp.float32
    )
    cols_energy = jnp.dot(
        one_hot, energy_table, precision=lax.Precision.HIGHEST, preferred_element_type=jnp.float32
    )
    ladder = lax.psum_scatter(
        partial_value.astype(jnp.bfloat16), "ksplit", scatter_dimension=0, tiled=True
    ).astype(jnp.float32)
    rows_energy = lax.dynamic_slice_in_dim(virt_energy, virt_index * rows_local, rows_local)
    denominator = rows_energy[None, :, None] + cols_energy[:, None, :] - pair_energy[:, None, None]
    updated = ((driving.astype(jnp.float32) + ladder) / denominator).astype(jnp.bfloat16)
    flipped = jnp.swapaxes(updated, 1, 2)
    return lax.all_to_all(flipped, "virt", split_axis=1, concat_axis=2, tiled=True)


def solution(mesh):
    placed = (
        P("virt", "ksplit"),
        P(("pair", "virt"), "ksplit", None, None, None),
        P(("pair", "virt"), "ksplit", None),
        P(("pair", "virt"), "ksplit"),
        P(("pair", "ksplit"), "virt", None),
        P(),
        P(("pair", "ksplit")),
        P(("pair", "ksplit")),
    )
    return jax.shard_map(
        body,
        mesh=mesh,
        in_specs=placed,
        out_specs=P(("pair", "ksplit"), "virt", None),
        check_vma=False,
    )
```

profile of v0, /device:TPU:0, one launch (start us, length us, event | category | flops | bytes accessed | tf_op | source)
XLA Modules:
  0.0 78.9 jit_solution(655376620068557921)
XLA Ops:
  6.5 0.0 all-gather.2.cloned.1.call-start
  6.5 0.7 all-gather.2.cloned.1.call-update
  7.3 0.0 reduce-scatter.2.cloned.1.call-start
  7.3 1.2 %dynamic-slice = u32[1]{0:T(128)} dynamic-slice(u32[32]{0:T(128)} %constant.40, u32[]{:T(128)S(6)} %add.51), dynamic_slice_sizes={1} | dynamic-slice | bytes 12
  9.2 0.8 bitcast_dynamic-update-slice_fusion
  10.0 9.9 %all-reduce = s32[8]{0:T(128)S(1)} all-reduce(s32[8]{0:T(128)S(1)} %bitcast_dynamic-update-slice_fusion), channel_id=1, replica_groups=mesh['pair'=4,'virt'=4,'ksplit'=2] {'virt'}, use_global_device_ids=true, to_apply=%add | all-reduce | flops 8 | bytes 64
  19.9 9.5 %all_gather.11 = s32[8,1,4]{2,1,0:T(1,128)S(1)} all-gather(s32[2,1,4]{2,1,0:T(1,128)} %param.10), channel_id=1, replica_groups=mesh['pair'=4,'virt'=4,'ksplit'=2] {'virt'}, dimensions={0}, use_global_device_ids=true | all-gather | bytes 160 | tf_op jit(solution)/shard_map/all_gather | solution.py:18
  29.3 0.1 copy.37
  29.4 0.1 copy.40
  29.5 0.1 reshape.65
  29.6 1.1 %copy.39 = bf16[256,512]{0,1:T(8,128)(2,1)S(1)} copy(bf16[256,512]{1,0:T(8,128)(2,1)} %param.8) | data formatting | bytes 524288 | tf_op args[0]
  30.7 0.2 copy.41
  30.9 0.1 copy.38
  31.0 1.0 %gather_fusion = bf16[32,256,128]{2,1,0:T(8,128)(2,1)S(1)} fusion(bf16[256,4,128]{2,0,1:T(8,128)(2,1)S(1)} %copy.41, s32[1024]{0:T(1024)S(1)} %pad_clamp_fusion), kind=kCustom, calls=%fused_computation | custom fusion | bytes 4194432 | tf_op jit(solution)/shard_map/jit(_take)/gather | solution.py:21
  31.9 0.1 iota_compare_fusion
  32.0 7.6 %all-gather.2.cloned.1.call-done = bf16[8,1,4,128,128]{4,3,2,1,0:T(8,128)(2,1)} async-done(((bf16[2,1,4,128,128]{4,3,2,1,0:T(8,128)(2,1)}), bf16[8,1,4,128,128]{4,3,2,1,0:T(8,128)(2,1)}) %all-gather.2.cloned.1.call-update) | async-done | bytes 1048592 | tf_op jit(solution)/shard_map/all_gather | solution.py:17
  39.6 0.0 copy-start.2
  39.6 0.0 copy-start.3
  39.6 0.0 copy-start
  39.6 2.9 %fusion.7 = bf16[8,256,128]{2,1,0:T(8,128)(2,1)} fusion(bf16[8,4,256,128]{3,2,1,0:T(8,128)(2,1)S(1)} %bitcast.38, pred[8,4]{1,0:T(8,128)(4,1)S(1)} %copy.38, bf16[8,1,4,128,128]{4,3,2,1,0:T(8,128)(2,1)} %all-gather.2.cloned.1.call-done, pred[8,4]{1,0:T(8,128)(4,1)S(1)} %iota_compare_fusion), kind=kOutput, calls=%fused_computation.6 | convolution fusion | flops 270270464 | bytes 3670080 | tf_op jit(solution)/shard_map/apsc,pscb->pab/dot_general | solution.py:24
  42.5 0.0 reduce-scatter.2.cloned.1.call-update
  42.5 0.0 copy-done.2
  42.5 0.1 dynamic_slice.3
  42.6 0.0 copy-done.3
  42.6 0.2 fusion.14
  42.8 13.9 %reduce-scatter.2.cloned.1.call-done = bf16[4,256,128]{2,1,0:T(8,128)(2,1)} async-done(((bf16[8,256,128]{2,1,0:T(8,128)(2,1)}), bf16[4,256,128]{2,1,0:T(8,128)(2,1)}) %reduce-scatter.2.cloned.1.call-update) | async-done | bytes 262160 | tf_op jit(solution)/shard_map/reduce_scatter | solution.py:33
  56.7 0.0 copy-done
  56.7 0.0 copy-done.1
  56.7 1.1 %fusion.13 = bf16[4,128,256]{1,2,0:T(8,128)(2,1)S(1)} fusion(f32[4]{0:T(128)S(1)} %copy-done.1, f32[4,128]{1,0:T(4,128)S(1)} %fusion.14, f32[256]{0:T(256)S(1)} %dynamic_slice.3, bf16[4,256,128]{2,1,0:T(8,128)(2,1)} %reduce-scatter.2.cloned.1.call-done, bf16[4,256,128]{2,1,0:T(8,128)(2,1)S(1)} %copy-done), kind=kLoop, calls=%fused_computation.12 | loop fusion | flops 917504 | bytes 789520 | tf_op jit(solution)/shard_map/transpose | solution.py:39
  57.9 0.2 copy.42
  58.1 13.3 %all_to_all.18 = bf16[4,128,256]{2,0,1:T(4,128)(2,1)S(1)} all-to-all(bf16[4,128,256]{2,0,1:T(4,128)(2,1)S(1)} %copy.42), channel_id=1, replica_groups=mesh['pair'=4,'virt'=4,'ksplit'=2] {'virt'}, dimensions={1} | all-to-all | bytes 524288 | tf_op jit(solution)/shard_map/all_to_all | solution.py:40
  71.4 0.7 copy.46
  (6 shorter events, 0.1 us)
Async XLA Ops:
  6.5 33.1 %all-gather.2.cloned.1.call-start = ((), (), s32[]{:S(2)}) async-start(), calls=%async_computation.2 | async-start | bytes 1310720 | tf_op jit(solution)/shard_map/all_gather | solution.py:17
  7.3 49.5 %reduce-scatter.2.cloned.1.call-start = ((), (), s32[]{:S(2)}) async-start(), calls=%async_computation.3 | async-start | bytes 786432 | tf_op jit(solution)/shard_map/reduce_scatter | solution.py:33
  39.6 2.9 %copy-start.2 = (f32[1024]{0:T(1024)S(1)}, f32[1024]{0:T(1024)}, u32[]{:S(2)}) copy-start(f32[1024]{0:T(1024)} %param.13) | copy-start | bytes 12292
  39.6 3.0 %copy-start.3 = (s32[4]{0:T(128)S(1)}, s32[4]{0:T(128)}, u32[]{:S(2)}) copy-start(s32[4]{0:T(128)} %param.15) | copy-start | bytes 52
  39.6 17.1 %copy-start = (bf16[4,256,128]{2,1,0:T(8,128)(2,1)S(1)}, bf16[4,256,128]{2,1,0:T(8,128)(2,1)}, u32[]{:S(2)}) copy-start(bf16[4,256,128]{2,1,0:T(8,128)(2,1)} %param.12) | copy-start | bytes 786436
  39.6 17.1 %copy-start.1 = (f32[4]{0:T(128)S(1)}, f32[4]{0:T(128)}, u32[]{:S(2)}) copy-start(f32[4]{0:T(128)} %param.14) | copy-start | bytes 52
Sparse Core Ops, SparseCore 0:
  8.9 30.6 all-gather.1
  42.6 14.0 reduce-scatter.1
where the time goes:
time: 79.2 us; the launch traced here: 78.9 us
  blocking collectives  32.6 us (41%)
  waiting for transfers between devices  22.3 us (28%)
  between operations  14.1 us (18%)
  local copies, waits for them, and re-layouts  5.59 us (7%)
  matrix products  3.04 us (4%)
  other arithmetic  1.23 us (2%)
    reduce_scatter x1, waiting for transfers between devices, body(): lax.psum_scatter(partial_value.astype(jnp.bfloat16), 'ksplit', scatter_di...  13.9 us
    all_to_all x1, blocking collectives, body(): lax.all_to_all(flipped, 'virt', split_axis=1, concat_axis=2, tiled=True)  13.3 us
    unnamed x1, blocking collectives  9.89 us
    all_gather x1, blocking collectives, body(): tiles = lax.all_gather(slot_tiles, 'virt', axis=0, tiled=True)  9.48 us
    all_gather x1, waiting for transfers between devices, body(): amps = lax.all_gather(amplitudes, 'virt', axis=0, tiled=True)  7.61 us
    unnamed x12, local copies, waits for them, and re-layouts  3.1 us
    dot_general x1, matrix products, body(): jnp.einsum('apsc,pscb->pab', chosen, masked, preferred_element_type=jnp.f...  2.86 us
  transfers between devices with their start and end apart: 2, of which 2 were waited for; matrix products, arithmetic and copies ran while one was open for 6% of the time, Pallas kernels for 0%

commit v1 on v0

--- a/solution.py
+++ b/solution.py
@@ -1,10 +1,16 @@
+import functools
+
 import jax
 import jax.numpy as jnp
 from jax import lax
+from jax.experimental import pallas as pl
+from jax.experimental.pallas import tpu as pltpu
 from jax.sharding import PartitionSpec as P
 
-
-def body(
+MESH = pl.DeviceIdType.MESH
+
+
+def gather_body(
     weights, amplitudes, slot_tiles, slot_counts, driving, virt_energy, pair_energy, pair_tile
 ):
     tile_width = amplitudes.shape[-1]
@@ -40,6 +46,281 @@
     return lax.all_to_all(flipped, "virt", split_axis=1, concat_axis=2, tiled=True)
 
 
+NQ, NV, NK = 4, 4, 2
+
+
+def kernel(
+    tiles_ref,
+    counts_ref,
+    pair_tile_ref,
+    pair_energy_ref,
+    w_hbm,
+    amps_hbm,
+    driving_hbm,
+    energy_ref,
+    out_ref,
+    w_all,
+    amps_in,
+    driving_in,
+    amps_tx,
+    amps_rx,
+    driving_tx,
+    driving_rx,
+    local_sem,
+    z_send,
+    z_recv,
+    y_send,
+    y_recv,
+    x_send,
+    x_recv,
+    c_send,
+    c_recv,
+    a_send,
+    a_recv,
+    d_send,
+    d_recv,
+):
+    q = lax.axis_index("pair")
+    v = lax.axis_index("virt")
+    y = lax.axis_index("ksplit")
+    other_y = 1 - y
+    core_q = q + 1 - 2 * lax.rem(q, 2)
+    far_q = lax.rem(q + 2, NQ)
+    far_core_q = lax.rem(core_q + 2, NQ)
+    pairs_in, slots, tile, _ = amps_in.shape
+    pairs_out = driving_in.shape[0]
+    chunk = tile // NV
+    block_tiles = amps_tx.shape[-1] // tile
+    rows_local = driving_in.shape[1]
+
+    w_load = pltpu.make_async_copy(w_hbm, w_all.at[y, v], local_sem.at[0])
+    amps_load = pltpu.make_async_copy(amps_hbm, amps_in, local_sem.at[1])
+    driving_load = pltpu.make_async_copy(driving_hbm, driving_in, local_sem.at[2])
+    w_load.start()
+    amps_load.start()
+    driving_load.start()
+
+    barrier = pltpu.get_barrier_semaphore()
+    peers = [(q, lax.rem(v + r, NV), y) for r in range(1, NV)]
+    peers += [(q, lax.rem(v + r, NV), other_y) for r in range(NV)]
+    peers += [(core_q, v, y), (far_q, v, y)]
+    for peer in peers:
+        pl.semaphore_signal(barrier, inc=1, device_id=peer, device_id_type=MESH)
+    pl.semaphore_wait(barrier, len(peers))
+
+    sent = []
+
+    def send(src, dst, send_sem, recv_sem, device):
+        copy = pltpu.make_async_remote_copy(
+            src_ref=src, dst_ref=dst, send_sem=send_sem, recv_sem=recv_sem,
+            device_id=device, device_id_type=MESH,
+        )
+        copy.start()
+        sent.append(copy)
+
+    def arrived(dst, sem):
+        pltpu.make_async_remote_copy(
+            src_ref=dst, dst_ref=dst, send_sem=sem, recv_sem=sem,
+            device_id=(core_q, v, y), device_id_type=MESH,
+        ).wait_recv()
+
+    def piece(split, virt, quarter):
+        return w_all.at[split, virt, quarter]
+
+    w_load.wait()
+    own = piece(y, v, q)
+    for r in (2, 1, 3):
+        send(own, own, z_send.at[r], z_recv.at[r], (q, lax.rem(v + r, NV), y))
+    send(own, own, y_send.at[0], y_recv.at[0], (q, v, other_y))
+
+    amps_load.wait()
+    for i in range(pairs_in):
+        count = counts_ref[i, 0]
+        loaded = [amps_in[i, s].astype(jnp.float32) for s in range(slots)]
+        for t in range(block_tiles):
+            total = jnp.zeros((tile, tile), jnp.float32)
+            for s in range(slots):
+                use = jnp.logical_and(count > s, tiles_ref[i, s] == y * block_tiles + t)
+                total = total + jnp.where(use, 1.0, 0.0).astype(jnp.float32) * loaded[s]
+            flipped = total.T.astype(jnp.bfloat16)
+            for j in range(NV):
+                amps_tx[j, i, :, t * tile:(t + 1) * tile] = flipped[j * chunk:(j + 1) * chunk]
+    owner_y = v // 2
+    half = lax.rem(v, 2)
+    a_slot = half * NK + y
+    a_dst = amps_rx.at[y, half]
+    for r in (2, 1, 3):
+        to = lax.rem(v + r, NV)
+        send(amps_tx.at[to], a_dst, a_send.at[r], a_recv.at[a_slot], (q, to, owner_y))
+
+    @pl.when(owner_y == y)
+    def _():
+        copy = pltpu.make_async_copy(amps_tx.at[v], a_dst, local_sem.at[1])
+        copy.start()
+        copy.wait()
+
+    @pl.when(owner_y != y)
+    def _():
+        pltpu.make_async_remote_copy(
+            src_ref=amps_tx.at[v], dst_ref=a_dst, send_sem=a_send.at[0], recv_sem=a_recv.at[a_slot],
+            device_id=(q, v, other_y), device_id_type=MESH,
+        ).start()
+
+    driving_load.wait()
+    for i in range(pairs_out):
+        for h in range(rows_local // tile):
+            flipped = driving_in[i, h * tile:(h + 1) * tile].astype(jnp.float32).T.astype(jnp.bfloat16)
+            for j in range(NV):
+                driving_tx[j, i, :, h * tile:(h + 1) * tile] = flipped[j * chunk:(j + 1) * chunk]
+    for r in (2, 1, 3):
+        to = lax.rem(v + r, NV)
+        send(driving_tx.at[to], driving_rx.at[v], d_send.at[r], d_recv.at[r], (q, to, y))
+    driving_own = pltpu.make_async_copy(driving_tx.at[v], driving_rx.at[v], local_sem.at[2])
+    driving_own.start()
+
+    order = (0, 1, 3, 2)
+    for r in order:
+        s = lax.rem(v + NV - r, NV)
+        if r:
+            got = piece(y, s, q)
+            arrived(got, z_recv.at[r])
+            send(got, got, y_send.at[r], y_recv.at[r], (q, v, other_y))
+            send(got, got, x_send.at[r, 0], x_recv.at[r, 0], (far_q, v, y))
+            send(got, got, c_send.at[r, 0, 0], c_recv.at[r, 0, 0], (core_q, v, y))
+    for r in order:
+        s = lax.rem(v + NV - r, NV)
+        got = piece(other_y, s, q)
+        arrived(got, y_recv.at[r])
+        send(got, got, x_send.at[r, 1], x_recv.at[r, 1], (far_q, v, y))
+        send(got, got, c_send.at[r, 1, 0], c_recv.at[r, 1, 0], (core_q, v, y))
+    for r in order:
+        s = lax.rem(v + NV - r, NV)
+        for n, split in ((0, y), (1, other_y)):
+            if r or n:
+                got = piece(split, s, far_q)
+                arrived(got, x_recv.at[r, n])
+                send(got, got, c_send.at[r, n, 1], c_recv.at[r, n, 1], (core_q, v, y))
+    for r in order:
+        s = lax.rem(v + NV - r, NV)
+        for n, split in ((0, y), (1, other_y)):
+            if r or n:
+                arrived(piece(split, s, core_q), c_recv.at[r, n, 0])
+                arrived(piece(split, s, far_core_q), c_recv.at[r, n, 1])
+
+    for src_half in range(2):
+        for src_y in range(NK):
+            slot = src_half * NK + src_y
+            mine = jnp.logical_and(v == y * 2 + src_half, y == src_y)
+
+            @pl.when(jnp.logical_not(mine))
+            def _():
+                arrived(amps_rx.at[src_y, src_half], a_recv.at[slot])
+
+    driving_own.wait()
+    for r in (1, 3, 2):
+        s = lax.rem(v + NV - r, NV)
+        arrived(driving_rx.at[s], d_recv.at[r])
+
+    rows = pairs_out * chunk
+    lane = lax.broadcasted_iota(jnp.int32, (chunk, tile), 1)
+    row = lax.broadcasted_iota(jnp.int32, (chunk, tile), 0)
+    picked = lane == row + v * chunk
+    shifts = []
+    for i in range(pairs_out):
+        line = energy_ref[pair_tile_ref[i]]
+        column = jnp.sum(jnp.where(picked, line, 0.0), axis=1, keepdims=True)
+        shifts.append((column, pair_energy_ref[i]))
+    left = [amps_rx[k].reshape(rows, amps_rx.shape[-1]) for k in range(NK)]
+    per_tile = rows_local // tile
+    for s in range(NV):
+        ladder = jnp.zeros((rows, rows_local), jnp.float32)
+        for k in range(NK):
+            block = w_all[k, s].reshape(rows_local, w_all.shape[-1])
+            ladder = ladder + lax.dot_general(
+                left[k], block, (((1,), (1,)), ((), ())), preferred_element_type=jnp.float32
+            )
+        for i in range(pairs_out):
+            column, pair = shifts[i]
+            for h in range(per_tile):
+                lanes = slice(h * tile, (h + 1) * tile)
+                denominator = energy_ref[s * per_tile + h] + column - pair
+                value = driving_rx[s, i, :, lanes].astype(jnp.float32)
+                value = value + ladder[i * chunk:(i + 1) * chunk, lanes]
+                out_ref[i, :, s * rows_local + h * tile:s * rows_local + (h + 1) * tile] = (
+                    value / denominator
+                ).astype(jnp.bfloat16)
+
+    for copy in sent:
+        copy.wait_send()
+
+    @pl.when(owner_y != y)
+    def _():
+        pltpu.make_async_remote_copy(
+            src_ref=amps_tx.at[v], dst_ref=a_dst, send_sem=a_send.at[0], recv_sem=a_recv.at[a_slot],
+            device_id=(q, v, other_y), device_id_type=MESH,
+        ).wait_send()
+
+
+def fused_body(
+    weights, amplitudes, slot_tiles, slot_counts, driving, virt_energy, pair_energy, pair_tile
+):
+    pairs_in, _, slots, tile, _ = amplitudes.shape
+    rows_local, columns = weights.shape
+    pairs_out = driving.shape[0]
+    chunk = tile // NV
+    whole_rows = virt_energy.shape[0]
+    bf16 = jnp.bfloat16
+    dma = pltpu.SemaphoreType.DMA
+    smem = pl.BlockSpec(memory_space=pltpu.SMEM)
+    hbm = pl.BlockSpec(memory_space=pl.ANY)
+    vmem = pl.BlockSpec(memory_space=pltpu.VMEM)
+    return pl.pallas_call(
+        kernel,
+        out_shape=jax.ShapeDtypeStruct((pairs_out, chunk, whole_rows), bf16),
+        in_specs=[smem, smem, smem, smem, hbm, hbm, hbm, vmem],
+        out_specs=vmem,
+        scratch_shapes=[
+            pltpu.VMEM((NK, NV, NQ, rows_local // NQ, columns), bf16),
+            pltpu.VMEM((pairs_in, slots, tile, tile), bf16),
+            pltpu.VMEM((pairs_out, rows_local, tile), bf16),
+            pltpu.VMEM((NV, pairs_in, chunk, columns), bf16),
+            pltpu.VMEM((NK, 2, pairs_in, chunk, columns), bf16),
+            pltpu.VMEM((NV, pairs_out, chunk, rows_local), bf16),
+            pltpu.VMEM((NV, pairs_out, chunk, rows_local), bf16),
+            dma((3,)),
+            dma((NV,)),
+            dma((NV,)),
+            dma((NV,)),
+            dma((NV,)),
+            dma((NV, 2)),
+            dma((NV, 2)),
+            dma((NV, 2, 2)),
+            dma((NV, 2, 2)),
+            dma((NV,)),
+            dma((2 * NK,)),
+            dma((NV,)),
+            dma((NV,)),
+        ],
+        compiler_params=pltpu.CompilerParams(
+            collective_id=0, has_side_effects=True, vmem_limit_bytes=24 * 1024 * 1024
+        ),
+        cost_estimate=pl.CostEstimate(
+            flops=2 * pairs_out * chunk * whole_rows * columns * NK,
+            bytes_accessed=4 * 2 * rows_local * columns,
+            transcendentals=0,
+        ),
+    )(
+        slot_tiles.reshape(pairs_in, slots),
+        slot_counts,
+        pair_tile,
+        pair_energy,
+        weights.reshape(NQ, rows_local // NQ, columns),
+        amplitudes.reshape(pairs_in, slots, tile, tile),
+        driving,
+        virt_energy.reshape(whole_rows // tile, 1, tile),
+    )
+
+
 def solution(mesh):
     placed = (
         P("virt", "ksplit"),
@@ -51,10 +332,19 @@
         P(("pair", "ksplit")),
         P(("pair", "ksplit")),
     )
-    return jax.shard_map(
-        body,
-        mesh=mesh,
-        in_specs=placed,
-        out_specs=P(("pair", "ksplit"), "virt", None),
-        check_vma=False,
-    )
+    sizes = dict(mesh.shape)
+    plan = (sizes["pair"], sizes["virt"], sizes["ksplit"]) == (NQ, NV, NK)
+
+    def chosen(weights, amplitudes, *rest):
+        slots, tile = amplitudes.shape[2], amplitudes.shape[3]
+        small = weights.size <= 2 ** 21 and weights.shape[1] == 2 * NK * 2 * tile
+        pairs = amplitudes.shape[0] == 2 * NQ * NV
+        return jax.shard_map(
+            fused_body if plan and small and pairs else gather_body,
+            mesh=mesh,
+            in_specs=placed,
+            out_specs=P(("pair", "ksplit"), "virt", None),
+            check_vma=False,
+        )(weights, amplitudes, *rest)
+
+    return chosen

time: 79.2 us -> 33.7 us (0.43)
  the two profiles are of different devices: /device:TPU:0 before, /device:TPU:9 now
where the time goes in v1:
time: 33.7 us; the launch traced here: 33.4 us
  Pallas kernels  28.5 us (85%)
  local copies, waits for them, and re-layouts  4.9 us (15%)
    pallas_call x1, Pallas kernels, fused_body(): pl.pallas_call(kernel, out_shape=jax.ShapeDtypeStruct((pairs_out, chunk,...  28.5 us
    unnamed x18, local copies, waits for them, and re-layouts  4.9 us

profile of v1, /device:TPU:9, one launch (start us, length us, event | category | flops | bytes accessed | tf_op | source)
XLA Modules:
  0.0 33.4 jit_solution(8456177451692783086)
XLA Ops:
  0.0 0.0 copy-start.3
  0.0 0.0 copy-start.7
  0.0 0.0 copy-start.6
  0.0 0.7 %copy-done.7 = s32[2,1]{0,1:T(1,128)S(1)} copy-done((s32[2,1]{0,1:T(1,128)S(1)}, s32[2,1]{0,1:T(1,128)}, u32[]{:S(2)}) %copy-start.7) | copy-done | bytes 32
  0.7 0.0 copy-start.4
  0.7 0.0 copy-start.5
  0.7 0.1 copy.9.counts_ref
  0.8 0.0 copy-done.3
  0.8 0.0 copy-done.6
  0.8 0.6 %copy-done.4 = s32[2,1,4]{2,1,0:T(1,128)S(1)} copy-done((s32[2,1,4]{2,1,0:T(1,128)S(1)}, s32[2,1,4]{2,1,0:T(1,128)}, u32[]{:S(2)}) %copy-start.4) | copy-done | bytes 56
  1.4 0.0 copy-done.5
  1.4 0.0 copy-start
  1.4 0.9 %copy-done = bf16[256,512]{1,0:T(8,128)(2,1)S(1)} copy-done((bf16[256,512]{1,0:T(8,128)(2,1)S(1)}, bf16[256,512]{1,0:T(8,128)(2,1)}, u32[]{:S(2)}) %copy-start) | copy-done | bytes 262168
  2.3 0.0 copy-start.1
  2.3 0.9 %copy-done.1 = bf16[2,1,4,128,128]{4,3,2,1,0:T(8,128)(2,1)S(1)} copy-done((bf16[2,1,4,128,128]{4,3,2,1,0:T(8,128)(2,1)S(1)}, bf16[2,1,4,128,128]{4,3,2,1,0:T(8,128)(2,1)}, u32[]{:S(2)}) %copy-start.1) | copy-done | bytes 262168
  3.3 0.0 copy-start.2
  3.3 0.9 %copy-done.2 = bf16[4,256,128]{2,1,0:T(8,128)(2,1)S(1)} copy-done((bf16[4,256,128]{2,1,0:T(8,128)(2,1)S(1)}, bf16[4,256,128]{2,1,0:T(8,128)(2,1)}, u32[]{:S(2)}) %copy-start.2) | copy-done | bytes 262168
  4.2 28.5 %shard_map.82 = bf16[4,32,1024]{2,1,0:T(8,128)(2,1)S(1)} custom-call(s32[2,4]{1,0:T(2,128)S(1)} %bitcast.7, s32[2,1]{1,0:T(2,128)S(1)} %copy.9.counts_ref, s32[4]{0:T(128)S(1)} %copy-done.5, f32[4]{0:T(128)S(1)} %copy-done.6, bf16[4,64,512]{2,1,0:T(8,128)(2,1)S(1)} %bitcast.4, bf16[2,4,128,128]{3,2,1,0:T(8,128)(2,1)S(1)} %bitcast.5, ...), custom_call_target="tpu_custom_call" | custom-call | flops 268435456 | bytes 1048576 | tf_op jit(solution)/shard_map/pallas_call | solution.py:277
  32.7 0.7 %copy.11 = bf16[4,32,1024]{2,1,0:T(8,128)(2,1)} copy(bf16[4,32,1024]{2,1,0:T(8,128)(2,1)S(1)} %shard_map.82) | data formatting | bytes 524288
Async XLA Ops:
  0.0 0.8 %copy-start.3 = (f32[1024]{0:T(1024)S(1)}, f32[1024]{0:T(1024)}, u32[]{:S(2)}) copy-start(f32[1024]{0:T(1024)} %param.13) | copy-start | bytes 12292
  0.0 0.7 %copy-start.7 = (s32[2,1]{0,1:T(1,128)S(1)}, s32[2,1]{0,1:T(1,128)}, u32[]{:S(2)}) copy-start(s32[2,1]{0,1:T(1,128)} %param.11) | copy-start | bytes 28
  0.0 0.8 %copy-start.6 = (f32[4]{0:T(128)S(1)}, f32[4]{0:T(128)}, u32[]{:S(2)}) copy-start(f32[4]{0:T(128)} %pair_energy_ref.1) | copy-start | bytes 52
  0.7 0.7 %copy-start.4 = (s32[2,1,4]{2,1,0:T(1,128)S(1)}, s32[2,1,4]{2,1,0:T(1,128)}, u32[]{:S(2)}) copy-start(s32[2,1,4]{2,1,0:T(1,128)} %param.10) | copy-start | bytes 100
  0.7 0.7 %copy-start.5 = (s32[4]{0:T(128)S(1)}, s32[4]{0:T(128)}, u32[]{:S(2)}) copy-start(s32[4]{0:T(128)} %pair_tile_ref.1) | copy-start | bytes 52
  1.4 1.0 %copy-start = (bf16[256,512]{1,0:T(8,128)(2,1)S(1)}, bf16[256,512]{1,0:T(8,128)(2,1)}, u32[]{:S(2)}) copy-start(bf16[256,512]{1,0:T(8,128)(2,1)} %param.8) | copy-start | bytes 786436
  2.3 0.9 %copy-start.1 = (bf16[2,1,4,128,128]{4,3,2,1,0:T(8,128)(2,1)S(1)}, bf16[2,1,4,128,128]{4,3,2,1,0:T(8,128)(2,1)}, u32[]{:S(2)}) copy-start(bf16[2,1,4,128,128]{4,3,2,1,0:T(8,128)(2,1)} %param.9) | copy-start | bytes 786436
  3.3 0.9 %copy-start.2 = (bf16[4,256,128]{2,1,0:T(8,128)(2,1)S(1)}, bf16[4,256,128]{2,1,0:T(8,128)(2,1)}, u32[]{:S(2)}) copy-start(bf16[4,256,128]{2,1,0:T(8,128)(2,1)} %driving_hbm.1) | copy-start | bytes 786436

commit v2 on v1

v2 whole, which is shorter than its diff:
```python
import jax
import jax.numpy as jnp
from jax import lax
from jax.experimental import pallas as pl
from jax.experimental.pallas import tpu as pltpu
from jax.sharding import PartitionSpec as P

MESH = pl.DeviceIdType.MESH


def gather_body(
    weights, amplitudes, slot_tiles, slot_counts, driving, virt_energy, pair_energy, pair_tile
):
    tile_width = amplitudes.shape[-1]
    slot_number = amplitudes.shape[2]
    rows_local = weights.shape[0]
    blocks_local = weights.shape[1] // tile_width
    split_index = lax.axis_index("ksplit")
    virt_index = lax.axis_index("virt")
    column_tiles = weights.reshape(rows_local, blocks_local, tile_width)
    amps = lax.all_gather(amplitudes, "virt", axis=0, tiled=True)
    tiles = lax.all_gather(slot_tiles, "virt", axis=0, tiled=True)
    counts = lax.all_gather(slot_counts, "virt", axis=0, tiled=True)
    local_ids = tiles[:, 0, :] - split_index * blocks_local
    chosen = jnp.take(column_tiles, local_ids, axis=1)
    live_slot = jnp.arange(slot_number, dtype=jnp.int32)[None, :] < counts
    masked = jnp.where(live_slot[:, :, None, None], amps[:, 0], jnp.zeros((), jnp.bfloat16))
    partial_value = jnp.einsum("apsc,pscb->pab", chosen, masked, preferred_element_type=jnp.float32)
    tile_count = virt_energy.shape[0] // tile_width
    energy_table = virt_energy.reshape(tile_count, tile_width)
    one_hot = (pair_tile[:, None] == jnp.arange(tile_count, dtype=jnp.int32)[None, :]).astype(
        jnp.float32
    )
    cols_energy = jnp.dot(
        one_hot, energy_table, precision=lax.Precision.HIGHEST, preferred_element_type=jnp.float32
    )
    ladder = lax.psum_scatter(
        partial_value.astype(jnp.bfloat16), "ksplit", scatter_dimension=0, tiled=True
    ).astype(jnp.float32)
    rows_energy = lax.dynamic_slice_in_dim(virt_energy, virt_index * rows_local, rows_local)
    denominator = rows_energy[None, :, None] + cols_energy[:, None, :] - pair_energy[:, None, None]
    updated = ((driving.astype(jnp.float32) + ladder) / denominator).astype(jnp.bfloat16)
    flipped = jnp.swapaxes(updated, 1, 2)
    return lax.all_to_all(flipped, "virt", split_axis=1, concat_axis=2, tiled=True)


NQ, NV, NK = 4, 4, 2


def kernel(
    tiles_hbm,
    counts_hbm,
    pair_tile_hbm,
    pair_energy_hbm,
    w_hbm,
    amps_hbm,
    driving_hbm,
    energy_hbm,
    out_ref,
    tiles_ref,
    counts_ref,
    pair_tile_ref,
    pair_energy_ref,
    energy_ref,
    w_all,
    amps_in,
    driving_in,
    amps_tx,
    amps_rx,
    driving_tx,
    driving_rx,
    ladder_ref,
    local_sem,
    z_send,
    z_recv,
    y_send,
    y_recv,
    x_send,
    x_recv,
    c_send,
    c_recv,
    a_send,
    a_recv,
    d_send,
    d_recv,
):
    q = lax.axis_index("pair")
    v = lax.axis_index("virt")
    y = lax.axis_index("ksplit")
    other_y = 1 - y
    core_q = q + 1 - 2 * lax.rem(q, 2)
    far_q = lax.rem(q + 2, NQ)
    far_core_q = lax.rem(core_q + 2, NQ)
    first = v + 1 - 2 * lax.rem(v, 2)
    second = 2 - v // 2
    third = 3 - 3 * (v // 2)
    inner = jnp.logical_or(v == 1, v == 2)
    pairs_in, slots, tile, _ = amps_in.shape
    pairs_out = driving_in.shape[0]
    chunk = tile // NV
    block_tiles = amps_tx.shape[-1] // tile
    rows_local = driving_in.shape[1]

    loads = [
        pltpu.make_async_copy(src, dst, local_sem.at[n])
        for n, (src, dst) in enumerate((
            (amps_hbm, amps_in),
            (w_hbm, w_all.at[y, v]),
            (tiles_hbm, tiles_ref),
            (counts_hbm, counts_ref),
            (driving_hbm, driving_in),
            (pair_tile_hbm, pair_tile_ref),
            (pair_energy_hbm, pair_energy_ref),
            (energy_hbm, energy_ref),
        ))
    ]
    for load in loads:
        load.start()
    amps_load, w_load, tiles_load, counts_load, driving_load, *other_loads = loads

    barrier = pltpu.get_barrier_semaphore()
    peers = [(q, lax.rem(v + r, NV), y) for r in range(1, NV)]
    peers += [(q, lax.rem(v + r, NV), other_y) for r in range(NV)]
    peers += [(core_q, v, y), (far_q, v, y)]
    for peer in peers:
        pl.semaphore_signal(barrier, inc=1, device_id=peer, device_id_type=MESH)
    w_load.wait()
    pl.semaphore_wait(barrier, len(peers))

    sent = []

    def send(src, dst, send_sem, recv_sem, device, when=None):
        copy = pltpu.make_async_remote_copy(
            src_ref=src, dst_ref=dst, send_sem=send_sem, recv_sem=recv_sem,
            device_id=device, device_id_type=MESH,
        )
        if when is None:
            copy.start()
        else:
            pl.when(when)(copy.start)
        sent.append((copy, when))

    def arrived(dst, sem):
        pltpu.make_async_remote_copy(
            src_ref=dst, dst_ref=dst, send_sem=sem, recv_sem=sem,
            device_id=(core_q, v, y), device_id_type=MESH,
        ).wait_recv()

    own = w_all.at[y, v, q]
    send(own, own, z_send.at[v, 1], z_recv.at[v], (q, second, y), inner)
    send(own, own, z_send.at[v, 0], z_recv.at[v], (q, first, y))
    send(own, own, y_send.at[v], y_recv.at[v], (q, v, other_y))

    amps_load.wait()
    tiles_load.wait()
    counts_load.wait()
    for i in range(pairs_in):
        count = counts_ref[i]
        loaded = [amps_in[i, s].astype(jnp.float32) for s in range(slots)]
        for t in range(block_tiles):
            total = jnp.zeros((tile, tile), jnp.float32)
            for s in range(slots):
                use = jnp.logical_and(count > s, tiles_ref[i, 0, s] == y * block_tiles + t)
                total = total + jnp.where(use, 1.0, 0.0).astype(jnp.float32) * loaded[s]
            flipped = total.T.astype(jnp.bfloat16)
            for j in range(NV):
                amps_tx[j, i, :, t * tile:(t + 1) * tile] = flipped[j * chunk:(j + 1) * chunk]
    owner_y = v // 2
    half = lax.rem(v, 2)
    a_slot = half * NK + y
    a_dst = amps_rx.at[y, half]
    for to in (third, second, first):
        send(amps_tx.at[to], a_dst, a_send.at[to], a_recv.at[a_slot], (q, to, owner_y))
    own_amps = pltpu.make_async_copy(amps_tx.at[v], a_dst, local_sem.at[0])
    pl.when(owner_y == y)(own_amps.start)
    send(amps_tx.at[v], a_dst, a_send.at[v], a_recv.at[a_slot], (q, v, other_y), owner_y != y)

    driving_load.wait()
    for i in range(pairs_out):
        for h in range(rows_local // tile):
            flipped = driving_in[i, h * tile:(h + 1) * tile].astype(jnp.float32).T.astype(jnp.bfloat16)
            for j in range(NV):
                driving_tx[j, i, :, h * tile:(h + 1) * tile] = flipped[j * chunk:(j + 1) * chunk]
    for to in (third, second, first):
        send(driving_tx.at[to], driving_rx.at[v], d_send.at[to], d_recv.at[v], (q, to, y))
    own_driving = pltpu.make_async_copy(driving_tx.at[v], driving_rx.at[v], local_sem.at[1])
    own_driving.start()

    def from_virt(s, to, when):
        got = w_all.at[y, s, q]
        arrived(got, z_recv.at[s])
        send(got, got, z_send.at[s, 0], z_recv.at[s], (q, to, y), when)
        send(got, got, y_send.at[s], y_recv.at[s], (q, v, other_y))
        send(got, got, x_send.at[s, 0], x_recv.at[s, 0], (far_q, v, y))
        send(got, got, c_send.at[s, 0, 0], c_recv.at[s, 0, 0], (core_q, v, y))

    def from_split(s):
        got = w_all.at[other_y, s, q]
        arrived(got, y_recv.at[s])
        send(got, got, x_send.at[s, 1], x_recv.at[s, 1], (far_q, v, y))
        send(got, got, c_send.at[s, 1, 0], c_recv.at[s, 1, 0], (core_q, v, y))

    def from_far(s, n):
        got = w_all.at[(y, other_y)[n], s, far_q]
        arrived(got, x_recv.at[s, n])
        send(got, got, c_send.at[s, n, 1], c_recv.at[s, n, 1], (core_q, v, y))

    from_virt(first, second, inner)
    from_split(v)
    from_virt(second, first, inner)
    from_split(first)
    from_far(v, 1)
    from_far(first, 0)
    from_virt(third, first, inner)
    from_split(second)
    from_far(first, 1)
    from_far(second, 0)
    from_split(third)
    from_far(second, 1)
    from_far(third, 0)
    from_far(third, 1)

    pl.when(owner_y == y)(own_amps.wait)
    for src_half in range(2):
        for src_y in range(NK):
            mine = jnp.logical_and(v == y * 2 + src_half, y == src_y)

            @pl.when(jnp.logical_not(mine))
            def _():
                arrived(amps_rx.at[src_y, src_half], a_recv.at[src_half * NK + src_y])

    rows = pairs_out * chunk
    left = [amps_rx[k].reshape(rows, amps_rx.shape[-1]) for k in range(NK)]
    for s in (v, first, second, third):
        for n in range(NK):
            if n or s is not v:
                split = (y, other_y)[n]
                arrived(w_all.at[split, s, core_q], c_recv.at[s, n, 0])
                arrived(w_all.at[split, s, far_core_q], c_recv.at[s, n, 1])
        ladder = jnp.zeros((rows, rows_local), jnp.float32)
        for k in range(NK):
            block = w_all[k, s].reshape(rows_local, w_all.shape[-1])
            ladder = ladder + lax.dot_general(
                left[k], block, (((1,), (1,)), ((), ())), preferred_element_type=jnp.float32
            )
        ladder_ref[s] = ladder

    for load in other_loads:
        load.wait()
    lane = lax.broadcasted_iota(jnp.int32, (chunk, tile), 1)
    row = lax.broadcasted_iota(jnp.int32, (chunk, tile), 0)
    picked = lane == row + v * chunk
    shifts = []
    for i in range(pairs_out):
        line = energy_ref[pair_tile_ref[i]]
        column = jnp.sum(jnp.where(picked, line, 0.0), axis=1, keepdims=True)
        shifts.append((column, pair_energy_ref[i]))
    per_tile = rows_local // tile
    own_driving.wait()
    for s in (first, second, third):
        arrived(driving_rx.at[s], d_recv.at[s])
    for s in range(NV):
        for i in range(pairs_out):
            column, pair = shifts[i]
            for h in range(per_tile):
                lanes = slice(h * tile, (h + 1) * tile)
                denominator = energy_ref[s * per_tile + h] + column - pair
                value = driving_rx[s, i, :, lanes].astype(jnp.float32)
                value = value + ladder_ref[s, i * chunk:(i + 1) * chunk, lanes]
                out_ref[i, :, s * rows_local + h * tile:s * rows_local + (h + 1) * tile] = (
                    value / denominator
                ).astype(jnp.bfloat16)

    for copy, when in sent:
        if when is None:
            copy.wait_send()
        else:
            pl.when(when)(copy.wait_send)


def fused_body(
    weights, amplitudes, slot_tiles, slot_counts, driving, virt_energy, pair_energy, pair_tile
):
    pairs_in, _, slots, tile, _ = amplitudes.shape
    rows_local, columns = weights.shape
    pairs_out = driving.shape[0]
    chunk = tile // NV
    whole_rows = virt_energy.shape[0]
    bf16 = jnp.bfloat16
    dma = pltpu.SemaphoreType.DMA
    hbm = pl.BlockSpec(memory_space=pltpu.HBM)
    return pl.pallas_call(
        kernel,
        out_shape=jax.ShapeDtypeStruct((pairs_out, chunk, whole_rows), bf16),
        in_specs=[hbm] * 8,
        out_specs=pl.BlockSpec(memory_space=pltpu.VMEM),
        scratch_shapes=[
            pltpu.SMEM((pairs_in, 1, slots), jnp.int32),
            pltpu.SMEM((pairs_in,), jnp.int32),
            pltpu.SMEM((pairs_out,), jnp.int32),
            pltpu.SMEM((pairs_out,), jnp.float32),
            pltpu.VMEM((whole_rows // tile, 1, tile), jnp.float32),
            pltpu.VMEM((NK, NV, NQ, rows_local // NQ, columns), bf16),
            pltpu.VMEM((pairs_in, slots, tile, tile), bf16),
            pltpu.VMEM((pairs_out, rows_local, tile), bf16),
            pltpu.VMEM((NV, pairs_in, chunk, columns), bf16),
            pltpu.VMEM((NK, 2, pairs_in, chunk, columns), bf16),
            pltpu.VMEM((NV, pairs_out, chunk, rows_local), bf16),
            pltpu.VMEM((NV, pairs_out, chunk, rows_local), bf16),
            pltpu.VMEM((NV, pairs_out * chunk, rows_local), jnp.float32),
            dma((8,)),
            dma((NV, 2)),
            dma((NV,)),
            dma((NV,)),
            dma((NV,)),
            dma((NV, 2)),
            dma((NV, 2)),
            dma((NV, 2, 2)),
            dma((NV, 2, 2)),
            dma((NV,)),
            dma((2 * NK,)),
            dma((NV,)),
            dma((NV,)),
        ],
        compiler_params=pltpu.CompilerParams(
            collective_id=0, has_side_effects=True, vmem_limit_bytes=56 * 1024 * 1024
        ),
        cost_estimate=pl.CostEstimate(
            flops=2 * pairs_out * chunk * whole_rows * columns * NK,
            bytes_accessed=4 * 2 * rows_local * columns,
            transcendentals=0,
        ),
    )(
        slot_tiles,
        slot_counts.reshape(pairs_in),
        pair_tile,
        pair_energy,
        weights.reshape(NQ, rows_local // NQ, columns),
        amplitudes.reshape(pairs_in, slots, tile, tile),
        driving,
        virt_energy.reshape(whole_rows // tile, 1, tile),
    )


def solution(mesh):
    placed = (
        P("virt", "ksplit"),
        P(("pair", "virt"), "ksplit", None, None, None),
        P(("pair", "virt"), "ksplit", None),
        P(("pair", "virt"), "ksplit"),
        P(("pair", "ksplit"), "virt", None),
        P(),
        P(("pair", "ksplit")),
        P(("pair", "ksplit")),
    )
    sizes = dict(mesh.shape)
    plan = (sizes["pair"], sizes["virt"], sizes["ksplit"]) == (NQ, NV, NK)

    def chosen(weights, amplitudes, *rest):
        slots, tile = amplitudes.shape[2], amplitudes.shape[3]
        small = weights.size <= 2 ** 21 and weights.shape[1] == 2 * NK * 2 * tile
        pairs = amplitudes.shape[0] == 2 * NQ * NV
        return jax.shard_map(
            fused_body if plan and small and pairs else gather_body,
            mesh=mesh,
            in_specs=placed,
            out_specs=P(("pair", "ksplit"), "virt", None),
            check_vma=False,
        )(weights, amplitudes, *rest)

    return chosen
```

time: 33.7 us -> 35.7 us (1.059)
  the two profiles are of different devices: /device:TPU:9 before, /device:TPU:0 now
where the time goes in v2:
time: 35.7 us; the launch traced here: 35.6 us
  Pallas kernels  33.9 us (95%)
  local copies, waits for them, and re-layouts  1.67 us (5%)
    pallas_call x1, Pallas kernels, fused_body(): pl.pallas_call(kernel, out_shape=jax.ShapeDtypeStruct((pairs_out, chunk,...  33.9 us
    unnamed x1, local copies, waits for them, and re-layouts  1.67 us

profile of v2, /device:TPU:0, one launch (start us, length us, event | category | flops | bytes accessed | tf_op | source)
XLA Modules:
  0.0 35.6 jit_solution(17789862156493166053)
XLA Ops:
  0.0 33.9 %shard_map.82 = bf16[4,32,1024]{2,1,0:T(8,128)(2,1)} custom-call(s32[2,1,4]{2,1,0:T(1,128)} %tiles_hbm.1, s32[2]{0:T(128)} %bitcast.7, s32[4]{0:T(128)} %pair_tile_hbm.1, f32[4]{0:T(128)} %pair_energy_hbm.1, bf16[4,64,512]{2,1,0:T(8,128)(2,1)} %bitcast.4, bf16[2,4,128,128]{3,2,1,0:T(8,128)(2,1)} %bitcast.5, bf16[4,256,128]{2,1,0:T(8,128)(2,1)} %driving_hbm.1, ...), custom_call_target="tpu_custom_call" | custom-call | flops 268435456 | bytes 1048576 | tf_op jit(solution)/shard_map/pallas_call | solution.py:292
  33.9 1.7 %copy.10 = bf16[4,32,1024]{2,1,0:T(8,128)(2,1)} copy(bf16[4,32,1024]{2,1,0:T(8,128)(2,1)} %shard_map.82) | data formatting | bytes 524288

commit v3 on v2

--- a/solution.py
+++ b/solution.py
@@ -94,7 +94,6 @@
     first = v + 1 - 2 * lax.rem(v, 2)
     second = 2 - v // 2
     third = 3 - 3 * (v // 2)
-    inner = jnp.logical_or(v == 1, v == 2)
     pairs_in, slots, tile, _ = amps_in.shape
     pairs_out = driving_in.shape[0]
     chunk = tile // NV
@@ -121,7 +120,7 @@
     barrier = pltpu.get_barrier_semaphore()
     peers = [(q, lax.rem(v + r, NV), y) for r in range(1, NV)]
     peers += [(q, lax.rem(v + r, NV), other_y) for r in range(NV)]
-    peers += [(core_q, v, y), (far_q, v, y)]
+    peers += [(core_q, v, y), (far_q, v, y), (far_q, v, other_y)]
     for peer in peers:
         pl.semaphore_signal(barrier, inc=1, device_id=peer, device_id_type=MESH)
     w_load.wait()
@@ -147,9 +146,10 @@
         ).wait_recv()
 
     own = w_all.at[y, v, q]
-    send(own, own, z_send.at[v, 1], z_recv.at[v], (q, second, y), inner)
-    send(own, own, z_send.at[v, 0], z_recv.at[v], (q, first, y))
+    for to in (first, second, third):
+        send(own, own, z_send.at[to], z_recv.at[v], (q, to, y))
     send(own, own, y_send.at[v], y_recv.at[v], (q, v, other_y))
+    send(own, own, x_send.at[v, 1], x_recv.at[v, 1], (far_q, v, other_y))
 
     amps_load.wait()
     tiles_load.wait()
@@ -175,6 +175,26 @@
     pl.when(owner_y == y)(own_amps.start)
     send(amps_tx.at[v], a_dst, a_send.at[v], a_recv.at[a_slot], (q, v, other_y), owner_y != y)
 
+    def from_virt(s):
+        got = w_all.at[y, s, q]
+        arrived(got, z_recv.at[s])
+        send(got, got, x_send.at[s, 0], x_recv.at[s, 0], (far_q, v, y))
+        send(got, got, x_send.at[s, 1], x_recv.at[s, 1], (far_q, v, other_y))
+        send(got, got, y_send.at[s], y_recv.at[s], (q, v, other_y))
+        send(got, got, c_send.at[s, 0, 0], c_recv.at[s, 0, 0], (core_q, v, y))
+
+    def from_split(s):
+        got = w_all.at[other_y, s, q]
+        arrived(got, y_recv.at[s])
+        send(got, got, c_send.at[s, 1, 0], c_recv.at[s, 1, 0], (core_q, v, y))
+
+    def from_far(s, n):
+        got = w_all.at[(y, other_y)[n], s, far_q]
+        arrived(got, x_recv.at[s, n])
+        send(got, got, c_send.at[s, n, 1], c_recv.at[s, n, 1], (core_q, v, y))
+
+    from_virt(first)
+
     driving_load.wait()
     for i in range(pairs_out):
         for h in range(rows_local // tile):
@@ -186,37 +206,17 @@
     own_driving = pltpu.make_async_copy(driving_tx.at[v], driving_rx.at[v], local_sem.at[1])
     own_driving.start()
 
-    def from_virt(s, to, when):
-        got = w_all.at[y, s, q]
-        arrived(got, z_recv.at[s])
-        send(got, got, z_send.at[s, 0], z_recv.at[s], (q, to, y), when)
-        send(got, got, y_send.at[s], y_recv.at[s], (q, v, other_y))
-        send(got, got, x_send.at[s, 0], x_recv.at[s, 0], (far_q, v, y))
-        send(got, got, c_send.at[s, 0, 0], c_recv.at[s, 0, 0], (core_q, v, y))
-
-    def from_split(s):
-        got = w_all.at[other_y, s, q]
-        arrived(got, y_recv.at[s])
-        send(got, got, x_send.at[s, 1], x_recv.at[s, 1], (far_q, v, y))
-        send(got, got, c_send.at[s, 1, 0], c_recv.at[s, 1, 0], (core_q, v, y))
-
-    def from_far(s, n):
-        got = w_all.at[(y, other_y)[n], s, far_q]
-        arrived(got, x_recv.at[s, n])
-        send(got, got, c_send.at[s, n, 1], c_recv.at[s, n, 1], (core_q, v, y))
-
-    from_virt(first, second, inner)
     from_split(v)
-    from_virt(second, first, inner)
+    from_far(v, 1)
+    from_virt(second)
     from_split(first)
-    from_far(v, 1)
     from_far(first, 0)
-    from_virt(third, first, inner)
+    from_far(first, 1)
+    from_virt(third)
     from_split(second)
-    from_far(first, 1)
     from_far(second, 0)
+    from_far(second, 1)
     from_split(third)
-    from_far(second, 1)
     from_far(third, 0)
     from_far(third, 1)
 
@@ -309,7 +309,7 @@
             pltpu.VMEM((NV, pairs_out, chunk, rows_local), bf16),
             pltpu.VMEM((NV, pairs_out * chunk, rows_local), jnp.float32),
             dma((8,)),
-            dma((NV, 2)),
+            dma((NV,)),
             dma((NV,)),
             dma((NV,)),
             dma((NV,)),

time: 35.7 us -> 30.1 us (0.84)
  Pallas kernels: 33.9 us -> 28.3 us
    pallas_call x1, Pallas kernels: 33.9 us -> 28.3 us  [fused_body(): pl.pallas_call(kernel, out_shape=jax.ShapeDtypeStruct((pairs_out, chunk,...]
where the time goes in v3:
time: 30.1 us; the launch traced here: 30 us
  Pallas kernels  28.3 us (94%)
  local copies, waits for them, and re-layouts  1.67 us (6%)
    pallas_call x1, Pallas kernels, fused_body(): pl.pallas_call(kernel, out_shape=jax.ShapeDtypeStruct((pairs_out, chunk,...  28.3 us
    unnamed x1, local copies, waits for them, and re-layouts  1.67 us

profile of v3, /device:TPU:0, one launch (start us, length us, event | category | flops | bytes accessed | tf_op | source)
XLA Modules:
  0.0 30.0 jit_solution(9857589414432687963)
XLA Ops:
  0.0 28.3 %shard_map.82 = bf16[4,32,1024]{2,1,0:T(8,128)(2,1)} custom-call(s32[2,1,4]{2,1,0:T(1,128)} %tiles_hbm.1, s32[2]{0:T(128)} %bitcast.7, s32[4]{0:T(128)} %pair_tile_hbm.1, f32[4]{0:T(128)} %pair_energy_hbm.1, bf16[4,64,512]{2,1,0:T(8,128)(2,1)} %bitcast.4, bf16[2,4,128,128]{3,2,1,0:T(8,128)(2,1)} %bitcast.5, bf16[4,256,128]{2,1,0:T(8,128)(2,1)} %driving_hbm.1, ...), custom_call_target="tpu_custom_call" | custom-call | flops 268435456 | bytes 1048576 | tf_op jit(solution)/shard_map/pallas_call | solution.py:292
  28.3 1.7 %copy.10 = bf16[4,32,1024]{2,1,0:T(8,128)(2,1)} copy(bf16[4,32,1024]{2,1,0:T(8,128)(2,1)} %shard_map.82) | data formatting | bytes 524288

commit v4 on v3

--- a/solution.py
+++ b/solution.py
@@ -56,7 +56,7 @@
     amps_hbm,
     driving_hbm,
     energy_hbm,
-    out_ref,
+    out_hbm,
     tiles_ref,
     counts_ref,
     pair_tile_ref,
@@ -70,6 +70,7 @@
     driving_tx,
     driving_rx,
     ladder_ref,
+    out_ref,
     local_sem,
     z_send,
     z_recv,
@@ -194,6 +195,8 @@
         send(got, got, c_send.at[s, n, 1], c_recv.at[s, n, 1], (core_q, v, y))
 
     from_virt(first)
+    from_virt(second)
+    from_virt(third)
 
     driving_load.wait()
     for i in range(pairs_out):
@@ -208,11 +211,9 @@
 
     from_split(v)
     from_far(v, 1)
-    from_virt(second)
     from_split(first)
     from_far(first, 0)
     from_far(first, 1)
-    from_virt(third)
     from_split(second)
     from_far(second, 0)
     from_far(second, 1)
@@ -259,8 +260,9 @@
     own_driving.wait()
     for s in (first, second, third):
         arrived(driving_rx.at[s], d_recv.at[s])
-    for s in range(NV):
-        for i in range(pairs_out):
+    stores = []
+    for i in range(pairs_out):
+        for s in range(NV):
             column, pair = shifts[i]
             for h in range(per_tile):
                 lanes = slice(h * tile, (h + 1) * tile)
@@ -270,7 +272,11 @@
                 out_ref[i, :, s * rows_local + h * tile:s * rows_local + (h + 1) * tile] = (
                     value / denominator
                 ).astype(jnp.bfloat16)
-
+        stores.append(pltpu.make_async_copy(out_ref.at[i], out_hbm.at[i], local_sem.at[2 + i]))
+        stores[-1].start()
+
+    for store in stores:
+        store.wait()
     for copy, when in sent:
         if when is None:
             copy.wait_send()
@@ -293,7 +299,7 @@
         kernel,
         out_shape=jax.ShapeDtypeStruct((pairs_out, chunk, whole_rows), bf16),
         in_specs=[hbm] * 8,
-        out_specs=pl.BlockSpec(memory_space=pltpu.VMEM),
+        out_specs=hbm,
         scratch_shapes=[
             pltpu.SMEM((pairs_in, 1, slots), jnp.int32),
             pltpu.SMEM((pairs_in,), jnp.int32),
@@ -308,6 +314,7 @@
             pltpu.VMEM((NV, pairs_out, chunk, rows_local), bf16),
             pltpu.VMEM((NV, pairs_out, chunk, rows_local), bf16),
             pltpu.VMEM((NV, pairs_out * chunk, rows_local), jnp.float32),
+            pltpu.VMEM((pairs_out, chunk, whole_rows), bf16),
             dma((8,)),
             dma((NV,)),
             dma((NV,)),

time: 30.1 us -> 29.1 us (0.967)
  Pallas kernels: 28.3 us -> 27.2 us
    pallas_call x1, Pallas kernels: 28.3 us -> 27.2 us  [fused_body(): pl.pallas_call(kernel, out_shape=jax.ShapeDtypeStruct((pairs_out, chunk,...]
where the time goes in v4:
time: 29.1 us; the launch traced here: 28.9 us
  Pallas kernels  27.2 us (93%)
  local copies, waits for them, and re-layouts  1.67 us (6%)
    pallas_call x1, Pallas kernels, fused_body(): pl.pallas_call(kernel, out_shape=jax.ShapeDtypeStruct((pairs_out, chunk,...  27.2 us
    unnamed x1, local copies, waits for them, and re-layouts  1.67 us

profile of v4, /device:TPU:0, one launch (start us, length us, event | category | flops | bytes accessed | tf_op | source)
XLA Modules:
  0.0 28.9 jit_solution(12840234619054833128)
XLA Ops:
  0.0 27.2 %shard_map.82 = bf16[4,32,1024]{2,1,0:T(8,128)(2,1)} custom-call(s32[2,1,4]{2,1,0:T(1,128)} %tiles_hbm.1, s32[2]{0:T(128)} %bitcast.7, s32[4]{0:T(128)} %pair_tile_hbm.1, f32[4]{0:T(128)} %pair_energy_hbm.1, bf16[4,64,512]{2,1,0:T(8,128)(2,1)} %bitcast.4, bf16[2,4,128,128]{3,2,1,0:T(8,128)(2,1)} %bitcast.5, bf16[4,256,128]{2,1,0:T(8,128)(2,1)} %driving_hbm.1, ...), custom_call_target="tpu_custom_call" | custom-call | flops 268435456 | bytes 1048576 | tf_op jit(solution)/shard_map/pallas_call | solution.py:298
  27.2 1.7 %copy.10 = bf16[4,32,1024]{2,1,0:T(8,128)(2,1)} copy(bf16[4,32,1024]{2,1,0:T(8,128)(2,1)} %shard_map.82) | data formatting | bytes 524288
